TPU v7x, 32 devices: a whole 2x2x4 slice. The times are simulated.
32 devices in a mesh: grp: 2 (over y), pix: 4 (over z), chan: 2 (over x), sub: 2 (over core).
Axes of the slice: x: 2, y: 2, z: 4, core: 2. Of those that a mesh axis runs over, the one named last changes fastest.
Arguments:
- features: bfloat16 [256, 131072], P('chan', ('grp', 'pix', 'sub')), parts along dimension 1, may hold values from -6 to 6
- neighbours: int32 [8, 131072], P(None, ('grp', 'pix', 'sub')), parts along dimension 1, may hold values from 0 to 8703, as said below
- live_cols: int32 [16], P(('grp', 'pix', 'sub')), parts along dimension 0, may hold values from 8 to 32, as said below
- cheb_weight: bfloat16 [7, 256, 256], replicated, may hold values from -0.125 to 0.125
- out_bias: float32 [256], replicated, may hold values from -3 to 3
Outputs:
- mixed: bfloat16 [16, 8192, 256], P(('grp', 'pix', 'sub'), 'chan'), parts along dimension 0
There are 2 independent parts, one for each index of `grp`. A program takes and returns all parts, laid end to end along the dimension named above; an argument that names none is the same for every part. Nothing has to cross between parts.
Inputs may be any that keep to these rules, and one draw needn't show every extreme that they name: `live_cols`: every patch has at least 8 live columns; some patch has all 32 columns live. `neighbours`: Entry t of a live slot at column c and latitude l names either the slot itself (extended index 256 + s) or the slot at column c + dc and latitude l + dl, with (dc, dl) = (-1,-1), (-1,0), (-1,1), (0,-1), (0,1), (1,-1), (1,0), (1,1) for t = 0 to 7; column -1 means the last live column of the previous patch and column live_cols[p] the first column of the next patch, and the latitude stays within 0 to 255. Dead slots name only themselves.
All inputs are finite; a program needn't handle non-finite values.
Results may differ from a plain program's by a relative error of at most 0.0039.
Values may be sent and summed in bfloat16 or wider, within the bound.
No kernel may reach another device: no remote copies, remote signals or barrier semaphores. Data moves between devices by JAX's collectives and lax.ppermute only.
A program may use at most 64 MiB of HBM per device.

v0:
```python
import jax
import jax.numpy as jnp
from jax import lax
from jax.sharding import PartitionSpec as P

DEG = 6
LATS = 256
tap_offsets = [(-1, -1), (-1, 0), (-1, 1), (0, -1), (0, 1), (1, -1), (1, 0), (1, 1)]


def shifted(value, axis, steps):
    count = lax.axis_size(axis)
    pairs = [(source, (source + steps) % count) for source in range(count)]
    return lax.ppermute(value, axis, pairs)


def tap_sum(padded, present, start, width):
    center = lax.slice_in_dim(padded, start, start + width, axis=1)
    summed = jnp.zeros(center.shape, jnp.float32)
    for tap_index in range(8):
        step_col, step_lat = tap_offsets[tap_index]
        moved_start = start + step_col * LATS + step_lat
        moved = lax.slice_in_dim(padded, moved_start, moved_start + width, axis=1)
        summed = summed + jnp.where(present[tap_index][None, :], moved, center)
    return -0.125 * summed


def rim_step(field, present, live):
    first_col = field[:, :LATS]
    last_col = lax.dynamic_slice_in_dim(field, (live - 1) * LATS, LATS, 1)
    from_prev = shifted(last_col, ("pix", "sub"), 1)
    from_next = shifted(first_col, ("pix", "sub"), -1)
    margin = LATS + 1
    channels = field.shape[0]
    padded = jnp.concatenate(
        [
            jnp.zeros((channels, margin), jnp.float32),
            from_prev,
            field,
            jnp.zeros((channels, LATS + margin), jnp.float32),
        ],
        axis=1,
    )
    padded = lax.dynamic_update_slice_in_dim(padded, from_next, margin + LATS + live * LATS, 1)
    return tap_sum(padded, present, margin + LATS, field.shape[1])


def shards(features, neighbours, live_cols, cheb_weight, out_bias):
    slot_count = features.shape[1]
    live = live_cols[0]
    own_slots = jnp.arange(slot_count, dtype=jnp.int32)[None, :]
    present = neighbours != LATS + own_slots
    terms = [features]
    older = features.astype(jnp.float32)
    newer = rim_step(older, present, live)
    terms.append(newer.astype(jnp.bfloat16))
    for degree in range(2, DEG + 1):
        upcoming = 2.0 * rim_step(newer, present, live) - older
        older, newer = (newer, upcoming)
        terms.append(newer.astype(jnp.bfloat16))
    share = slot_count // lax.axis_size("chan")
    summed = jnp.zeros((share, cheb_weight.shape[2]), jnp.float32)
    for degree in range(DEG + 1):
        piece = lax.all_to_all(terms[degree], "chan", split_axis=1, concat_axis=0, tiled=True)
        summed = summed + jnp.einsum(
            "ip,io->po", piece, cheb_weight[degree], preferred_element_type=jnp.float32
        )
    slots = lax.axis_index("chan") * share + jnp.arange(share, dtype=jnp.int32)
    alive = slots < live * LATS
    result = jnp.where(alive[:, None], summed + out_bias[None, :], 0.0)
    return result.astype(jnp.bfloat16).reshape(1, share, cheb_weight.shape[2])


def solution(mesh):
    in_specs = (
        P("chan", ("grp", "pix", "sub")),
        P(None, ("grp", "pix", "sub")),
        P(("grp", "pix", "sub")),
        P(),
        P(),
    )
    out_specs = P(("grp", "pix", "sub"), "chan", None)
    return jax.shard_map(shards, mesh=mesh, in_specs=in_specs, out_specs=out_specs, check_vma=False)
```

profile of v0, /device:TPU:0, one launch (start us, length us, event | category | flops | bytes accessed | tf_op | source)
XLA Modules:
  0.0 369.9 jit_solution(14855939197385692050)
XLA Ops:
  0.0 4.1 %copy.6 = bf16[128,8192]{0,1:T(8,128)(2,1)} copy(bf16[128,8192]{1,0:T(8,128)(2,1)} %param.5) | data formatting | bytes 4194304 | tf_op args[0]
  4.1 3.9 %convert_element_type.24 = f32[128,8192]{0,1:T(8,128)} convert(bf16[128,8192]{0,1:T(8,128)(2,1)} %copy.6) | non-fusion elementwise | flops 1048576 | bytes 6291456 | tf_op jit(solution)/shard_map/convert_element_type | solution.py:54
  10.9 4.1 %collective-permute-start.1 = (f32[128,256]{0,1:T(8,128)S(1)}, f32[128,256]{0,1:T(8,128)S(1)}, u32[]{:S(2)}, u32[]{:S(2)}) collective-permute-start(f32[128,256]{0,1:T(8,128)S(1)} %slice.341), channel_id=1, source_target_pairs={{0,13},{1,0},{4,1},{5,4},{8,5},{9,8},{12,9},{13,12},{2,15},{3,2},{... | collective-permute-start | bytes 393224 | tf_op jit(solution)/shard_map/ppermute | solution.py:14
  16.7 14.2 %concatenate.18 = f32[128,9218]{0,1:T(8,128)} concatenate(f32[128,257]{0,1:T(8,128)S(1)} %broadcast.29, f32[128,256]{0,1:T(8,128)S(1)} %collective-permute-done, bf16[128,8192]{0,1:T(8,128)(2,1)} %copy.6, f32[128,513]{0,1:T(8,128)S(1)} %broadcast.30), dimensions={1} | concatenate | bytes 7342080 | tf_op jit(solution)/shard_map/concatenate | solution.py:35
  32.6 20.4 %fusion.81 = (bf16[128,8192]{0,1:T(8,128)(2,1)}, f32[128,8192]{0,1:T(8,128)S(1)}) fusion(f32[128,9218]{0,1:T(8,128)} %dynamic_update_slice.18, pred[8192]{0:T(1024)(128)(4,1)S(1)} %get-tuple-element.6, pred[8192]{0:T(1024)(128)(4,1)S(1)} %get-tuple-element.7, pred[8192]{0:T(1024)(128)(4,1)S(1)} %get-tuple-element.8, ...), kind=kLoop, calls=%fused_computation.148 | loop fusion | flops 17825792 | bytes 44105728 | tf_op jit(solution)/shard_map/convert_element_type | solution.py:56
  53.0 2.1 copy-done.3
  55.2 3.5 collective-permute-start.3
  58.7 3.8 %all-to-all-start = ((bf16[128,2,4096]{0,2,1:T(8,128)(2,1)}), bf16[128,2,4096]{0,2,1:T(8,128)(2,1)S(1)}, u32[]{:S(2)}, u32[]{:S(2)}) async-start(bf16[128,2,4096]{0,2,1:T(8,128)(2,1)} %bitcast.1), calls=%async_computation | async-start | bytes 4194304 | tf_op jit(solution)/shard_map/all_to_all | solution.py:64
  62.5 14.5 %concatenate.19 = f32[128,9218]{0,1:T(8,128)} concatenate(f32[128,257]{0,1:T(8,128)S(1)} %broadcast.29, f32[128,256]{0,1:T(8,128)S(1)} %collective-permute-done.2, f32[128,8192]{0,1:T(8,128)} %copy-done.3, f32[128,513]{0,1:T(8,128)S(1)} %broadcast.30), dimensions={1} | concatenate | bytes 9439232 | tf_op jit(solution)/shard_map/concatenate | solution.py:35
  78.7 20.9 %fusion.79 = (bf16[128,8192]{0,1:T(8,128)(2,1)}, f32[128,8192]{0,1:T(8,128)S(1)}) fusion(bf16[128,8192]{0,1:T(8,128)(2,1)} %copy.6, f32[128,9218]{0,1:T(8,128)} %dynamic_update_slice.19, pred[8192]{0:T(1024)(128)(4,1)S(1)} %get-tuple-element.6, pred[8192]{0:T(1024)(128)(4,1)S(1)} %get-tuple-element.7, pred[8192]{0:T(1024)(128)(4,1)S(1)} %get-tuple-element.8, ...), kind=kLoop, calls=%fused_computation.147 | loop fusion | flops 19922944 | bytes 46202880 | tf_op jit(solution)/shard_map/convert_element_type | solution.py:60
  101.6 3.5 collective-permute-start.5
  105.1 3.1 collective-permute-done.4
  108.2 14.5 %concatenate.20 = f32[128,9218]{0,1:T(8,128)} concatenate(f32[128,257]{0,1:T(8,128)S(1)} %broadcast.29, f32[128,256]{0,1:T(8,128)S(1)} %collective-permute-done.4, f32[128,8192]{0,1:T(8,128)} %copy-done.2, f32[128,513]{0,1:T(8,128)S(1)} %broadcast.30), dimensions={1} | concatenate | bytes 9439232 | tf_op jit(solution)/shard_map/concatenate | solution.py:35
  124.4 4.8 %all-to-all-start.1 = ((bf16[128,2,4096]{0,2,1:T(8,128)(2,1)}), bf16[128,2,4096]{0,2,1:T(8,128)(2,1)}, u32[]{:S(2)}, u32[]{:S(2)}) async-start(bf16[128,2,4096]{0,2,1:T(8,128)(2,1)} %bitcast.64), calls=%async_computation.1 | async-start | bytes 4194304 | tf_op jit(solution)/shard_map/all_to_all | solution.py:64
  129.2 21.3 %fusion.77 = (bf16[128,8192]{0,1:T(8,128)(2,1)}, f32[128,8192]{0,1:T(8,128)S(1)}) fusion(f32[128,8192]{0,1:T(8,128)} %copy-done.3, f32[128,9218]{0,1:T(8,128)} %dynamic_update_slice.20, pred[8192]{0:T(1024)(128)(4,1)S(1)} %get-tuple-element.6, pred[8192]{0:T(1024)(128)(4,1)S(1)} %get-tuple-element.7, pred[8192]{0:T(1024)(128)(4,1)S(1)} %get-tuple-element.8, ...), kind=kLoop, calls=%fused_computation.146 | loop fusion | flops 18874368 | bytes 48300032 | tf_op jit(solution)/shard_map/convert_element_type | solution.py:60
  150.5 2.1 copy-done
  152.7 3.5 collective-permute-start.7
  156.2 2.6 collective-permute-done.6
  158.9 14.5 %concatenate.21 = f32[128,9218]{0,1:T(8,128)} concatenate(f32[128,257]{0,1:T(8,128)S(1)} %broadcast.29, f32[128,256]{0,1:T(8,128)S(1)} %collective-permute-done.6, f32[128,8192]{0,1:T(8,128)} %copy-done, f32[128,513]{0,1:T(8,128)S(1)} %broadcast.30), dimensions={1} | concatenate | bytes 9439232 | tf_op jit(solution)/shard_map/concatenate | solution.py:35
  175.0 3.8 %all-to-all-start.2 = ((bf16[128,2,4096]{0,2,1:T(8,128)(2,1)}), bf16[128,2,4096]{0,2,1:T(8,128)(2,1)S(1)}, u32[]{:S(2)}, u32[]{:S(2)}) async-start(bf16[128,2,4096]{0,2,1:T(8,128)(2,1)} %bitcast.10), calls=%async_computation.2 | async-start | bytes 4194304 | tf_op jit(solution)/shard_map/all_to_all | solution.py:64
  178.8 21.2 %fusion.75 = (bf16[128,8192]{0,1:T(8,128)(2,1)}, f32[128,8192]{0,1:T(8,128)S(1)}) fusion(f32[128,8192]{0,1:T(8,128)} %copy-done.2, f32[128,9218]{0,1:T(8,128)} %dynamic_update_slice.21, pred[8192]{0:T(1024)(128)(4,1)S(1)} %get-tuple-element.6, pred[8192]{0:T(1024)(128)(4,1)S(1)} %get-tuple-element.7, pred[8192]{0:T(1024)(128)(4,1)S(1)} %get-tuple-element.8, ...), kind=kLoop, calls=%fused_computation.145 | loop fusion | flops 18874368 | bytes 48300032 | tf_op jit(solution)/shard_map/convert_element_type | solution.py:60
  202.1 3.5 collective-permute-start.9
  205.6 2.6 collective-permute-done.8
  208.3 14.5 %concatenate.22 = f32[128,9218]{0,1:T(8,128)} concatenate(f32[128,257]{0,1:T(8,128)S(1)} %broadcast.29, f32[128,256]{0,1:T(8,128)S(1)} %collective-permute-done.8, f32[128,8192]{0,1:T(8,128)} %copy-done.1, f32[128,513]{0,1:T(8,128)S(1)} %broadcast.30), dimensions={1} | concatenate | bytes 9439232 | tf_op jit(solution)/shard_map/concatenate | solution.py:35
  224.4 4.8 %all-to-all-start.3 = ((bf16[128,2,4096]{0,2,1:T(8,128)(2,1)}), bf16[128,2,4096]{0,2,1:T(8,128)(2,1)}, u32[]{:S(2)}, u32[]{:S(2)}) async-start(bf16[128,2,4096]{0,2,1:T(8,128)(2,1)} %bitcast.14), calls=%async_computation.3 | async-start | bytes 4194304 | tf_op jit(solution)/shard_map/all_to_all | solution.py:64
  229.3 21.4 %fusion.73 = (bf16[128,8192]{0,1:T(8,128)(2,1)}, f32[128,8192]{0,1:T(8,128)S(1)}) fusion(f32[128,8192]{0,1:T(8,128)} %copy-done, f32[128,9218]{0,1:T(8,128)} %dynamic_update_slice.22, pred[8192]{0:T(1024)(128)(4,1)S(1)} %get-tuple-element.6, pred[8192]{0:T(1024)(128)(4,1)S(1)} %get-tuple-element.7, pred[8192]{0:T(1024)(128)(4,1)S(1)} %get-tuple-element.8, ...), kind=kLoop, calls=%fused_computation.144 | loop fusion | flops 18874368 | bytes 48300032 | tf_op jit(solution)/shard_map/convert_element_type | solution.py:60
  250.7 2.1 copy-done.4
  252.8 3.5 collective-permute-start.11
  256.4 2.6 collective-permute-done.10
  259.0 14.5 %concatenate.23 = f32[128,9218]{0,1:T(8,128)} concatenate(f32[128,257]{0,1:T(8,128)S(1)} %broadcast.29, f32[128,256]{0,1:T(8,128)S(1)} %collective-permute-done.10, f32[128,8192]{0,1:T(8,128)} %copy-done.4, f32[128,513]{0,1:T(8,128)S(1)} %broadcast.30), dimensions={1} | concatenate | bytes 9439232 | tf_op jit(solution)/shard_map/concatenate | solution.py:35
  275.2 4.8 %all-to-all-start.4 = ((bf16[128,2,4096]{0,2,1:T(8,128)(2,1)}), bf16[128,2,4096]{0,2,1:T(8,128)(2,1)}, u32[]{:S(2)}, u32[]{:S(2)}) async-start(bf16[128,2,4096]{0,2,1:T(8,128)(2,1)} %bitcast.18), calls=%async_computation.4 | async-start | bytes 4194304 | tf_op jit(solution)/shard_map/all_to_all | solution.py:64
  280.0 21.2 %fusion.7 = bf16[128,8192]{0,1:T(8,128)(2,1)} fusion(f32[128,8192]{0,1:T(8,128)} %copy-done.1, f32[128,9218]{0,1:T(8,128)} %dynamic_update_slice.23, pred[8192]{0:T(1024)(128)(4,1)S(1)} %get-tuple-element.6, pred[8192]{0:T(1024)(128)(4,1)S(1)} %get-tuple-element.7, pred[8192]{0:T(1024)(128)(4,1)S(1)} %get-tuple-element.8, ...), kind=kLoop, calls=%fused_computation.14 | loop fusion | flops 18874368 | bytes 44105728 | tf_op jit(solution)/shard_map/convert_element_type | solution.py:60
  301.2 3.0 copy.7
  304.2 5.0 %all-to-all-start.5 = ((bf16[128,2,4096]{0,2,1:T(8,128)(2,1)}), bf16[128,2,4096]{0,2,1:T(8,128)(2,1)}, u32[]{:S(2)}, u32[]{:S(2)}) async-start(bf16[128,2,4096]{0,2,1:T(8,128)(2,1)} %bitcast.54), calls=%async_computation.5 | async-start | bytes 4194304 | tf_op jit(solution)/shard_map/all_to_all | solution.py:64
  309.2 2.7 fusion.64
  311.9 4.1 %copy.9 = bf16[2,128,4096]{2,1,0:T(8,128)(2,1)} copy(bf16[2,128,4096]{1,2,0:T(8,128)(2,1)} %bitcast.7) | data formatting | bytes 4194304 | tf_op jit(solution)/shard_map/all_to_all | solution.py:64
  316.0 5.7 %convolution_add_fusion.5 = f32[4096,256]{1,0:T(8,128)} fusion(f32[4096,256]{1,0:T(8,128)} %fusion.64, bf16[256,4096]{1,0:T(8,128)(2,1)} %bitcast.60, bf16[7,256,256]{2,1,0:T(8,128)(2,1)S(1)} %copy-done.8), kind=kOutput, calls=%fused_computation.7 | convolution fusion | flops 537919488 | bytes 10616832 | tf_op jit(solution)/shard_map/ip,io->po/dot_general | solution.py:65
  321.7 2.7 copy.10
  324.4 5.5 %convolution_add_fusion.4 = f32[4096,256]{1,0:T(8,128)} fusion(f32[4096,256]{1,0:T(8,128)} %convolution_add_fusion.5, bf16[256,4096]{1,0:T(8,128)(2,1)} %bitcast.61, bf16[7,256,256]{2,1,0:T(8,128)(2,1)S(1)} %copy-done.8), kind=kOutput, calls=%fused_computation.6 | convolution fusion | flops 537919488 | bytes 10616832 | tf_op jit(solution)/shard_map/ip,io->po/dot_general | solution.py:65
  329.9 4.1 %copy.11 = bf16[2,128,4096]{2,1,0:T(8,128)(2,1)} copy(bf16[2,128,4096]{1,2,0:T(8,128)(2,1)} %bitcast.15) | data formatting | bytes 4194304 | tf_op jit(solution)/shard_map/all_to_all | solution.py:64
  334.0 3.8 %all-to-all-start.6 = ((bf16[128,2,4096]{0,2,1:T(8,128)(2,1)}), bf16[128,2,4096]{0,2,1:T(8,128)(2,1)S(1)}, u32[]{:S(2)}, u32[]{:S(2)}) async-start(bf16[128,2,4096]{0,2,1:T(8,128)(2,1)} %bitcast.65), calls=%async_computation.6 | async-start | bytes 4194304 | tf_op jit(solution)/shard_map/all_to_all | solution.py:64
  337.8 5.5 %convolution_add_fusion.3 = f32[4096,256]{1,0:T(8,128)} fusion(f32[4096,256]{1,0:T(8,128)} %convolution_add_fusion.4, bf16[256,4096]{1,0:T(8,128)(2,1)} %bitcast.58, bf16[7,256,256]{2,1,0:T(8,128)(2,1)S(1)} %copy-done.8), kind=kOutput, calls=%fused_computation.5 | convolution fusion | flops 537919488 | bytes 10616832 | tf_op jit(solution)/shard_map/ip,io->po/dot_general | solution.py:65
  343.3 4.1 %copy.12 = bf16[2,128,4096]{2,1,0:T(8,128)(2,1)} copy(bf16[2,128,4096]{1,2,0:T(8,128)(2,1)} %bitcast.19) | data formatting | bytes 4194304 | tf_op jit(solution)/shard_map/all_to_all | solution.py:64
  347.4 5.5 %convolution_add_fusion.2 = f32[4096,256]{1,0:T(8,128)} fusion(f32[4096,256]{1,0:T(8,128)} %convolution_add_fusion.3, bf16[256,4096]{1,0:T(8,128)(2,1)} %bitcast.62, bf16[7,256,256]{2,1,0:T(8,128)(2,1)S(1)} %copy-done.8), kind=kOutput, calls=%fused_computation.4 | convolution fusion | flops 537919488 | bytes 10616832 | tf_op jit(solution)/shard_map/ip,io->po/dot_general | solution.py:65
  352.9 4.1 %copy.13 = bf16[2,128,4096]{2,1,0:T(8,128)(2,1)} copy(bf16[2,128,4096]{1,2,0:T(8,128)(2,1)} %bitcast.23) | data formatting | bytes 4194304 | tf_op jit(solution)/shard_map/all_to_all | solution.py:64
  357.0 5.5 %convolution_add_fusion.1 = f32[4096,256]{1,0:T(8,128)} fusion(f32[4096,256]{1,0:T(8,128)} %convolution_add_fusion.2, bf16[256,4096]{1,0:T(8,128)(2,1)} %bitcast.63, bf16[7,256,256]{2,1,0:T(8,128)(2,1)S(1)} %copy-done.8), kind=kOutput, calls=%fused_computation.3 | convolution fusion | flops 537919488 | bytes 10616832 | tf_op jit(solution)/shard_map/ip,io->po/dot_general | solution.py:65
  362.5 2.8 copy.14
  365.3 4.5 %fusion.3 = bf16[1,4096,256]{2,1,0:T(8,128)(2,1)} fusion(f32[4096,256]{1,0:T(8,128)} %convolution_add_fusion.1, bf16[256,4096]{1,0:T(8,128)(2,1)} %bitcast.59, f32[256]{0:T(256)S(1)} %copy-done.10, pred[4096]{0:T(1024)(128)(4,1)S(1)} %add_compare_fusion, bf16[7,256,256]{2,1,0:T(8,128)(2,1)S(1)} %copy-done.8), kind=kOutput, calls=%fused_computation.9 | convolution fusion | flops 541065216 | bytes 8524800 | tf_op jit(solution)/shard_map/ip,io->po/dot_general | solution.py:65
  (59 shorter events, 18.5 us)
Async XLA Ops:
  4.1 10.9 %copy-start.9 = (s32[8,8192]{1,0:T(8,128)S(1)}, s32[8,8192]{1,0:T(8,128)}, u32[]{:S(2)}) copy-start(s32[8,8192]{1,0:T(8,128)} %param.6) | copy-start | bytes 786436
  9.5 7.2 %collective-permute-start = (f32[128,256]{0,1:T(8,128)S(1)}, f32[128,256]{0,1:T(8,128)S(1)}, u32[]{:S(2)}, u32[]{:S(2)}) collective-permute-start(f32[128,256]{0,1:T(8,128)S(1)} %constant_dynamic-slice_fusion.5), channel_id=1, source_target_pairs={{0,1},{1,4},{4,5},{5,8},{8,9},{9,12},{12,13},{13,0},{2,3},{3,6},{6... | collective-permute-start | bytes 393224 | tf_op jit(solution)/shard_map/ppermute | solution.py:14
  10.9 20.1 %collective-permute-start.1 = (f32[128,256]{0,1:T(8,128)S(1)}, f32[128,256]{0,1:T(8,128)S(1)}, u32[]{:S(2)}, u32[]{:S(2)}) collective-permute-start(f32[128,256]{0,1:T(8,128)S(1)} %slice.341), channel_id=1, source_target_pairs={{0,13},{1,0},{4,1},{5,4},{8,5},{9,8},{12,9},{13,12},{2,15},{3,2},{... | collective-permute-start | bytes 393224 | tf_op jit(solution)/shard_map/ppermute | solution.py:14
  53.0 2.1 copy-start.3
  55.1 7.4 %collective-permute-start.2 = (f32[128,256]{0,1:T(8,128)S(1)}, f32[128,256]{0,1:T(8,128)S(1)}, u32[]{:S(2)}, u32[]{:S(2)}) collective-permute-start(f32[128,256]{0,1:T(8,128)S(1)} %get-tuple-element.32), channel_id=1, source_target_pairs={{0,1},{1,4},{4,5},{5,8},{8,9},{9,12},{12,13},{13,0},{2,3},{3,6},{6... | collective-permute-start | bytes 393224 | tf_op jit(solution)/shard_map/ppermute | solution.py:14
  55.2 21.8 %collective-permute-start.3 = (f32[128,256]{0,1:T(8,128)S(1)}, f32[128,256]{0,1:T(8,128)S(1)}, u32[]{:S(2)}, u32[]{:S(2)}) collective-permute-start(f32[128,256]{0,1:T(8,128)S(1)} %get-tuple-element.31), channel_id=1, source_target_pairs={{0,13},{1,0},{4,1},{5,4},{8,5},{9,8},{12,9},{13,12},{2,15},{3,2},{... | collective-permute-start | bytes 393224 | tf_op jit(solution)/shard_map/ppermute | solution.py:14
  58.7 65.7 %all-to-all-start = ((bf16[128,2,4096]{0,2,1:T(8,128)(2,1)}), bf16[128,2,4096]{0,2,1:T(8,128)(2,1)S(1)}, u32[]{:S(2)}, u32[]{:S(2)}) async-start(bf16[128,2,4096]{0,2,1:T(8,128)(2,1)} %bitcast.1), calls=%async_computation | async-start | bytes 4194304 | tf_op jit(solution)/shard_map/all_to_all | solution.py:64
  99.5 2.0 copy-start.2
  101.5 6.6 %collective-permute-start.4 = (f32[128,256]{0,1:T(8,128)S(1)}, f32[128,256]{0,1:T(8,128)S(1)}, u32[]{:S(2)}, u32[]{:S(2)}) collective-permute-start(f32[128,256]{0,1:T(8,128)S(1)} %get-tuple-element.30), channel_id=1, source_target_pairs={{0,1},{1,4},{4,5},{5,8},{8,9},{9,12},{12,13},{13,0},{2,3},{3,6},{6... | collective-permute-start | bytes 393224 | tf_op jit(solution)/shard_map/ppermute | solution.py:14
  101.6 21.1 %collective-permute-start.5 = (f32[128,256]{0,1:T(8,128)S(1)}, f32[128,256]{0,1:T(8,128)S(1)}, u32[]{:S(2)}, u32[]{:S(2)}) collective-permute-start(f32[128,256]{0,1:T(8,128)S(1)} %get-tuple-element.29), channel_id=1, source_target_pairs={{0,13},{1,0},{4,1},{5,4},{8,5},{9,8},{12,9},{13,12},{2,15},{3,2},{... | collective-permute-start | bytes 393224 | tf_op jit(solution)/shard_map/ppermute | solution.py:14
  124.4 26.2 %copy-start.5 = (bf16[128,2,4096]{0,2,1:T(8,128)(2,1)}, bf16[128,2,4096]{0,2,1:T(8,128)(2,1)S(1)}, u32[]{:S(2)}) copy-start(bf16[128,2,4096]{0,2,1:T(8,128)(2,1)S(1)} %all-to-all-done) | copy-start | bytes 6291460
  124.4 50.7 %all-to-all-start.1 = ((bf16[128,2,4096]{0,2,1:T(8,128)(2,1)}), bf16[128,2,4096]{0,2,1:T(8,128)(2,1)}, u32[]{:S(2)}, u32[]{:S(2)}) async-start(bf16[128,2,4096]{0,2,1:T(8,128)(2,1)} %bitcast.64), calls=%async_computation.1 | async-start | bytes 4194304 | tf_op jit(solution)/shard_map/all_to_all | solution.py:64
  150.5 2.1 copy-start
  152.6 6.2 %collective-permute-start.6 = (f32[128,256]{0,1:T(8,128)S(1)}, f32[128,256]{0,1:T(8,128)S(1)}, u32[]{:S(2)}, u32[]{:S(2)}) collective-permute-start(f32[128,256]{0,1:T(8,128)S(1)} %get-tuple-element.28), channel_id=1, source_target_pairs={{0,1},{1,4},{4,5},{5,8},{8,9},{9,12},{12,13},{13,0},{2,3},{3,6},{6... | collective-permute-start | bytes 393224 | tf_op jit(solution)/shard_map/ppermute | solution.py:14
  152.7 20.7 %collective-permute-start.7 = (f32[128,256]{0,1:T(8,128)S(1)}, f32[128,256]{0,1:T(8,128)S(1)}, u32[]{:S(2)}, u32[]{:S(2)}) collective-permute-start(f32[128,256]{0,1:T(8,128)S(1)} %get-tuple-element.27), channel_id=1, source_target_pairs={{0,13},{1,0},{4,1},{5,4},{8,5},{9,8},{12,9},{13,12},{2,15},{3,2},{... | collective-permute-start | bytes 393224 | tf_op jit(solution)/shard_map/ppermute | solution.py:14
  175.0 49.4 %all-to-all-start.2 = ((bf16[128,2,4096]{0,2,1:T(8,128)(2,1)}), bf16[128,2,4096]{0,2,1:T(8,128)(2,1)S(1)}, u32[]{:S(2)}, u32[]{:S(2)}) async-start(bf16[128,2,4096]{0,2,1:T(8,128)(2,1)} %bitcast.10), calls=%async_computation.2 | async-start | bytes 4194304 | tf_op jit(solution)/shard_map/all_to_all | solution.py:64
  200.0 2.0 copy-start.1
  202.0 6.2 %collective-permute-start.8 = (f32[128,256]{0,1:T(8,128)S(1)}, f32[128,256]{0,1:T(8,128)S(1)}, u32[]{:S(2)}, u32[]{:S(2)}) collective-permute-start(f32[128,256]{0,1:T(8,128)S(1)} %get-tuple-element.26), channel_id=1, source_target_pairs={{0,1},{1,4},{4,5},{5,8},{8,9},{9,12},{12,13},{13,0},{2,3},{3,6},{6... | collective-permute-start | bytes 393224 | tf_op jit(solution)/shard_map/ppermute | solution.py:14
  202.1 20.7 %collective-permute-start.9 = (f32[128,256]{0,1:T(8,128)S(1)}, f32[128,256]{0,1:T(8,128)S(1)}, u32[]{:S(2)}, u32[]{:S(2)}) collective-permute-start(f32[128,256]{0,1:T(8,128)S(1)} %get-tuple-element.25), channel_id=1, source_target_pairs={{0,13},{1,0},{4,1},{5,4},{8,5},{9,8},{12,9},{13,12},{2,15},{3,2},{... | collective-permute-start | bytes 393224 | tf_op jit(solution)/shard_map/ppermute | solution.py:14
  224.4 26.2 %copy-start.6 = (bf16[128,2,4096]{0,2,1:T(8,128)(2,1)}, bf16[128,2,4096]{0,2,1:T(8,128)(2,1)S(1)}, u32[]{:S(2)}) copy-start(bf16[128,2,4096]{0,2,1:T(8,128)(2,1)S(1)} %all-to-all-done.2) | copy-start | bytes 6291460
  224.4 50.7 %all-to-all-start.3 = ((bf16[128,2,4096]{0,2,1:T(8,128)(2,1)}), bf16[128,2,4096]{0,2,1:T(8,128)(2,1)}, u32[]{:S(2)}, u32[]{:S(2)}) async-start(bf16[128,2,4096]{0,2,1:T(8,128)(2,1)} %bitcast.14), calls=%async_computation.3 | async-start | bytes 4194304 | tf_op jit(solution)/shard_map/all_to_all | solution.py:64
  250.7 2.1 copy-start.4
  252.7 6.2 %collective-permute-start.10 = (f32[128,256]{0,1:T(8,128)S(1)}, f32[128,256]{0,1:T(8,128)S(1)}, u32[]{:S(2)}, u32[]{:S(2)}) collective-permute-start(f32[128,256]{0,1:T(8,128)S(1)} %get-tuple-element.24), channel_id=1, source_target_pairs={{0,1},{1,4},{4,5},{5,8},{8,9},{9,12},{12,13},{13,0},{2,3},{3,6},{6... | collective-permute-start | bytes 393224 | tf_op jit(solution)/shard_map/ppermute | solution.py:14
  252.8 20.7 %collective-permute-start.11 = (f32[128,256]{0,1:T(8,128)S(1)}, f32[128,256]{0,1:T(8,128)S(1)}, u32[]{:S(2)}, u32[]{:S(2)}) collective-permute-start(f32[128,256]{0,1:T(8,128)S(1)} %get-tuple-element.23), channel_id=1, source_target_pairs={{0,13},{1,0},{4,1},{5,4},{8,5},{9,8},{12,9},{13,12},{2,15},{3,2},{... | collective-permute-start | bytes 393224 | tf_op jit(solution)/shard_map/ppermute | solution.py:14
  275.2 29.0 %all-to-all-start.4 = ((bf16[128,2,4096]{0,2,1:T(8,128)(2,1)}), bf16[128,2,4096]{0,2,1:T(8,128)(2,1)}, u32[]{:S(2)}, u32[]{:S(2)}) async-start(bf16[128,2,4096]{0,2,1:T(8,128)(2,1)} %bitcast.18), calls=%async_computation.4 | async-start | bytes 4194304 | tf_op jit(solution)/shard_map/all_to_all | solution.py:64
  301.1 8.0 %copy-start.8 = (bf16[7,256,256]{2,1,0:T(8,128)(2,1)S(1)}, bf16[7,256,256]{2,1,0:T(8,128)(2,1)}, u32[]{:S(2)}) copy-start(bf16[7,256,256]{2,1,0:T(8,128)(2,1)} %param.8) | copy-start | bytes 2752516
  304.2 29.8 %all-to-all-start.5 = ((bf16[128,2,4096]{0,2,1:T(8,128)(2,1)}), bf16[128,2,4096]{0,2,1:T(8,128)(2,1)}, u32[]{:S(2)}, u32[]{:S(2)}) async-start(bf16[128,2,4096]{0,2,1:T(8,128)(2,1)} %bitcast.54), calls=%async_computation.5 | async-start | bytes 4194304 | tf_op jit(solution)/shard_map/all_to_all | solution.py:64
  316.0 5.7 %copy-start.7 = (bf16[128,2,4096]{0,2,1:T(8,128)(2,1)S(1)}, bf16[128,2,4096]{0,2,1:T(8,128)(2,1)}, u32[]{:S(2)}) copy-start(bf16[128,2,4096]{0,2,1:T(8,128)(2,1)} %copy-done.6) | copy-start | bytes 6291460
  334.0 28.6 %all-to-all-start.6 = ((bf16[128,2,4096]{0,2,1:T(8,128)(2,1)}), bf16[128,2,4096]{0,2,1:T(8,128)(2,1)S(1)}, u32[]{:S(2)}, u32[]{:S(2)}) async-start(bf16[128,2,4096]{0,2,1:T(8,128)(2,1)} %bitcast.65), calls=%async_computation.6 | async-start | bytes 4194304 | tf_op jit(solution)/shard_map/all_to_all | solution.py:64
  362.5 2.8 copy-start.10
where the time goes:
time: 373 us; the launch traced here: 370 us
  local copies, waits for them, and re-layouts  138 us (37%)
  other arithmetic  130 us (35%)
  starting transfers between devices  53.3 us (14%)
  matrix products  35.1 us (9%)
  waiting for transfers between devices  12 us (3%)
    convert_element_type x6, other arithmetic, shards(): terms.append(newer.astype(jnp.bfloat16))  126 us
    concatenate x6, local copies, waits for them, and re-layouts, rim_step(): jnp.concatenate([jnp.zeros((channels, margin), jnp.float32), from_prev, f...  86.6 us
    dot_general x7, matrix products, shards(): jnp.einsum('ip,io->po', piece, cheb_weight[degree], preferred_element_typ...  35.1 us
    all_to_all x7, starting transfers between devices, shards(): lax.all_to_all(terms[degree], 'chan', split_axis=1, concat_axis=0, tiled=...  30.7 us
    all_to_all x7, local copies, waits for them, and re-layouts, shards(): lax.all_to_all(terms[degree], 'chan', split_axis=1, concat_axis=0, tiled=...  24.8 us
    ppermute x12, starting transfers between devices, shifted(): return lax.ppermute(value, axis, pairs)  22.6 us
    unnamed x23, local copies, waits for them, and re-layouts  14.2 us
    ppermute x12, waiting for transfers between devices, shifted(): return lax.ppermute(value, axis, pairs)  12 us
  transfers between devices with their start and end apart: 19, of which 5 were waited for; matrix products, arithmetic and copies ran while one was open for 69% of the time, Pallas kernels for 0%

commit v1 on v0

--- a/solution.py
+++ b/solution.py
@@ -1,3 +1,4 @@
+import functools
 import jax
 import jax.numpy as jnp
 from jax import lax
@@ -6,6 +7,16 @@
 DEG = 6
 LATS = 256
 tap_offsets = [(-1, -1), (-1, 0), (-1, 1), (0, -1), (0, 1), (1, -1), (1, 0), (1, 1)]
+
+
+def track_units(block_in, shard_axis):
+    taken_in = jax.lax.axis_size(shard_axis)
+    e_next = jnp.split(block_in, taken_in, axis=1)
+    d_next = jnp.stack(e_next)
+    return jnp.concatenate(jax.lax.all_to_all(d_next, shard_axis, 0, 0), axis=0)
+
+
+arrange_forms_now = functools.partial(track_units, shard_axis="chan")
 
 
 def shifted(value, axis, steps):
@@ -61,7 +72,7 @@
     share = slot_count // lax.axis_size("chan")
     summed = jnp.zeros((share, cheb_weight.shape[2]), jnp.float32)
     for degree in range(DEG + 1):
-        piece = lax.all_to_all(terms[degree], "chan", split_axis=1, concat_axis=0, tiled=True)
+        piece = arrange_forms_now(terms[degree])
         summed = summed + jnp.einsum(
             "ip,io->po", piece, cheb_weight[degree], preferred_element_type=jnp.float32
         )

time: 373 us -> 341 us (0.914)
  the two profiles are of different devices: /device:TPU:0 before, /device:TPU:28 now
where the time goes in v1:
time: 341 us; the launch traced here: 339 us
  other arithmetic  123 us (36%)
  waiting for transfers between devices  76.9 us (23%)
  local copies, waits for them, and re-layouts  64.7 us (19%)
  starting transfers between devices  50.3 us (15%)
  matrix products  23.5 us (7%)
    convert_element_type x6, other arithmetic, shards(): terms.append(newer.astype(jnp.bfloat16))  110 us
    all_to_all x7, waiting for transfers between devices, track_units(): return jnp.concatenate(jax.lax.all_to_all(d_next, shard_axis, 0, 0), axis=0)  72.8 us
    concatenate x6, local copies, waits for them, and re-layouts, rim_step(): jnp.concatenate([jnp.zeros((channels, margin), jnp.float32), from_prev, f...  38 us
    all_to_all x7, starting transfers between devices, track_units(): return jnp.concatenate(jax.lax.all_to_all(d_next, shard_axis, 0, 0), axis=0)  33.2 us
    dot_general x7, matrix products, shards(): jnp.einsum('ip,io->po', piece, cheb_weight[degree], preferred_element_typ...  23.5 us
    ppermute x12, starting transfers between devices, shifted(): return lax.ppermute(value, axis, pairs)  17.2 us
    another operation x7, local copies, waits for them, and re-layouts, track_units(): d_next = jnp.stack(e_next)  11.8 us
    dynamic_update_slice x6, local copies, waits for them, and re-layouts, rim_step(): lax.dynamic_update_slice_in_dim(padded, from_next, margin + LATS + live *...  11.1 us
  transfers between devices with their start and end apart: 19, of which 9 were waited for; matrix products, arithmetic and copies ran while one was open for 59% of the time, Pallas kernels for 0%

profile of v1, /device:TPU:28, one launch (start us, length us, event | category | flops | bytes accessed | tf_op | source)
XLA Modules:
  0.0 339.1 jit_solution(10171591011631306809)
XLA Ops:
  3.2 4.8 %all-to-all-start = ((bf16[2,128,4096]{2,1,0:T(8,128)(2,1)}), bf16[2,128,4096]{2,1,0:T(8,128)(2,1)}, u32[]{:S(2)}, u32[]{:S(2)}) async-start(bf16[2,128,4096]{2,1,0:T(8,128)(2,1)} %pad_maximum_fusion), calls=%async_computation | async-start | bytes 4194304 | tf_op jit(solution)/shard_map/all_to_all | solution.py:16
  8.0 2.4 convert_element_type.24
  12.1 1.8 collective-permute-start.1
  14.6 1.8 collective-permute-done
  16.5 4.3 %concatenate.18 = f32[128,9218]{1,0:T(8,128)} concatenate(f32[128,257]{1,0:T(8,128)S(1)} %broadcast.29, f32[128,256]{1,0:T(8,128)S(1)} %collective-permute-done, bf16[128,8192]{1,0:T(8,128)(2,1)S(1)} %copy-done.4, f32[128,513]{1,0:T(8,128)S(1)} %broadcast.30), dimensions={1} | concatenate | bytes 7342080 | tf_op jit(solution)/shard_map/concatenate | solution.py:46
  20.8 1.8 dynamic_update_slice.18
  22.7 16.7 %fusion.81 = (bf16[128,8192]{1,0:T(8,128)(2,1)S(1)}, f32[128,8192]{1,0:T(8,128)S(1)}) fusion(f32[128,9218]{1,0:T(8,128)} %dynamic_update_slice.18, pred[8192]{0:T(1024)(128)(4,1)S(1)} %get-tuple-element.6, pred[8192]{0:T(1024)(128)(4,1)S(1)} %get-tuple-element.7, pred[8192]{0:T(1024)(128)(4,1)S(1)} %get-tuple-element.8, ...), kind=kLoop, calls=%fused_computation.169 | loop fusion | flops 17825792 | bytes 44105728 | tf_op jit(solution)/shard_map/convert_element_type | solution.py:67
  39.7 1.7 collective-permute-start.3
  44.1 6.7 %concatenate.19 = f32[128,9218]{1,0:T(8,128)} concatenate(f32[128,257]{1,0:T(8,128)S(1)} %broadcast.29, f32[128,256]{1,0:T(8,128)S(1)} %collective-permute-done.2, f32[128,8192]{1,0:T(8,128)} %copy-done.3, f32[128,513]{1,0:T(8,128)S(1)} %broadcast.30), dimensions={1} | concatenate | bytes 9439232 | tf_op jit(solution)/shard_map/concatenate | solution.py:46
  50.8 1.8 dynamic_update_slice.19
  52.6 17.7 %fusion.79 = (bf16[128,8192]{1,0:T(8,128)(2,1)}, f32[128,8192]{1,0:T(8,128)S(1)}) fusion(bf16[128,8192]{1,0:T(8,128)(2,1)S(1)} %copy-done.4, f32[128,9218]{1,0:T(8,128)} %dynamic_update_slice.19, pred[8192]{0:T(1024)(128)(4,1)S(1)} %get-tuple-element.6, pred[8192]{0:T(1024)(128)(4,1)S(1)} %get-tuple-element.7, pred[8192]{0:T(1024)(128)(4,1)S(1)} %get-tuple-element.8, ...), kind=kLoop, calls=%fused_computation.168 | loop fusion | flops 19922944 | bytes 46202880 | tf_op jit(solution)/shard_map/convert_element_type | solution.py:71
  70.3 3.2 slice_bitcast_fusion.9
  78.0 6.7 %concatenate.20 = f32[128,9218]{1,0:T(8,128)} concatenate(f32[128,257]{1,0:T(8,128)S(1)} %broadcast.29, f32[128,256]{1,0:T(8,128)S(1)} %collective-permute-done.4, f32[128,8192]{1,0:T(8,128)} %copy-done.2, f32[128,513]{1,0:T(8,128)S(1)} %broadcast.30), dimensions={1} | concatenate | bytes 9439232 | tf_op jit(solution)/shard_map/concatenate | solution.py:46
  84.7 1.8 dynamic_update_slice.20
  86.6 18.7 %fusion.77 = (bf16[128,8192]{1,0:T(8,128)(2,1)}, f32[128,8192]{1,0:T(8,128)S(1)}) fusion(f32[128,8192]{1,0:T(8,128)} %copy-done.3, f32[128,9218]{1,0:T(8,128)} %dynamic_update_slice.20, pred[8192]{0:T(1024)(128)(4,1)S(1)} %get-tuple-element.6, pred[8192]{0:T(1024)(128)(4,1)S(1)} %get-tuple-element.7, pred[8192]{0:T(1024)(128)(4,1)S(1)} %get-tuple-element.8, ...), kind=kLoop, calls=%fused_computation.167 | loop fusion | flops 18874368 | bytes 48300032 | tf_op jit(solution)/shard_map/convert_element_type | solution.py:71
  105.3 3.2 slice_bitcast_fusion.7
  108.6 2.8 collective-permute-start.6
  113.0 6.7 %concatenate.21 = f32[128,9218]{1,0:T(8,128)} concatenate(f32[128,257]{1,0:T(8,128)S(1)} %broadcast.29, f32[128,256]{1,0:T(8,128)S(1)} %collective-permute-done.6, f32[128,8192]{1,0:T(8,128)} %copy-done, f32[128,513]{1,0:T(8,128)S(1)} %broadcast.30), dimensions={1} | concatenate | bytes 9439232 | tf_op jit(solution)/shard_map/concatenate | solution.py:46
  119.7 1.8 dynamic_update_slice.21
  121.6 18.9 %fusion.75 = (bf16[128,8192]{1,0:T(8,128)(2,1)}, f32[128,8192]{1,0:T(8,128)S(1)}) fusion(f32[128,8192]{1,0:T(8,128)} %copy-done.2, f32[128,9218]{1,0:T(8,128)} %dynamic_update_slice.21, pred[8192]{0:T(1024)(128)(4,1)S(1)} %get-tuple-element.6, pred[8192]{0:T(1024)(128)(4,1)S(1)} %get-tuple-element.7, pred[8192]{0:T(1024)(128)(4,1)S(1)} %get-tuple-element.8, ...), kind=kLoop, calls=%fused_computation.166 | loop fusion | flops 18874368 | bytes 48300032 | tf_op jit(solution)/shard_map/convert_element_type | solution.py:71
  140.5 4.6 %collective-permute-start.8 = (f32[128,256]{1,0:T(8,128)S(1)}, f32[128,256]{1,0:T(8,128)S(1)}, u32[]{:S(2)}, u32[]{:S(2)}) collective-permute-start(f32[128,256]{1,0:T(8,128)S(1)} %get-tuple-element.26), channel_id=1, source_target_pairs={{0,1},{1,4},{4,5},{5,8},{8,9},{9,12},{12,13},{13,0},{2,3},{3,6},{6... | collective-permute-start | bytes 393224 | tf_op jit(solution)/shard_map/ppermute | solution.py:25
  148.3 6.8 %concatenate.22 = f32[128,9218]{1,0:T(8,128)} concatenate(f32[128,257]{1,0:T(8,128)S(1)} %broadcast.29, f32[128,256]{1,0:T(8,128)S(1)} %collective-permute-done.8, f32[128,8192]{1,0:T(8,128)} %copy-done.1, f32[128,513]{1,0:T(8,128)S(1)} %broadcast.30), dimensions={1} | concatenate | bytes 9439232 | tf_op jit(solution)/shard_map/concatenate | solution.py:46
  155.1 1.8 dynamic_update_slice.22
  156.9 5.0 %all-to-all-start.1 = ((bf16[2,128,4096]{2,1,0:T(8,128)(2,1)}), bf16[2,128,4096]{2,1,0:T(8,128)(2,1)}, u32[]{:S(2)}, u32[]{:S(2)}) async-start(bf16[2,128,4096]{2,1,0:T(8,128)(2,1)} %pad_maximum_fusion.1), calls=%async_computation.1 | async-start | bytes 4194304 | tf_op jit(solution)/shard_map/all_to_all | solution.py:16
  162.0 18.7 %fusion.73 = (bf16[128,8192]{1,0:T(8,128)(2,1)}, f32[128,8192]{1,0:T(8,128)S(1)}) fusion(f32[128,8192]{1,0:T(8,128)} %copy-done, f32[128,9218]{1,0:T(8,128)} %dynamic_update_slice.22, pred[8192]{0:T(1024)(128)(4,1)S(1)} %get-tuple-element.6, pred[8192]{0:T(1024)(128)(4,1)S(1)} %get-tuple-element.7, pred[8192]{0:T(1024)(128)(4,1)S(1)} %get-tuple-element.8, ...), kind=kLoop, calls=%fused_computation.165 | loop fusion | flops 18874368 | bytes 48300032 | tf_op jit(solution)/shard_map/convert_element_type | solution.py:71
  180.7 2.1 copy-done.5
  182.8 4.3 %collective-permute-start.10 = (f32[128,256]{1,0:T(8,128)S(1)}, f32[128,256]{1,0:T(8,128)S(1)}, u32[]{:S(2)}, u32[]{:S(2)}) collective-permute-start(f32[128,256]{1,0:T(8,128)S(1)} %get-tuple-element.24), channel_id=1, source_target_pairs={{0,1},{1,4},{4,5},{5,8},{8,9},{9,12},{12,13},{13,0},{2,3},{3,6},{6... | collective-permute-start | bytes 393224 | tf_op jit(solution)/shard_map/ppermute | solution.py:25
  187.1 4.8 %all-to-all-start.2 = ((bf16[2,128,4096]{2,1,0:T(8,128)(2,1)}), bf16[2,128,4096]{2,1,0:T(8,128)(2,1)}, u32[]{:S(2)}, u32[]{:S(2)}) async-start(bf16[2,128,4096]{2,1,0:T(8,128)(2,1)} %pad_maximum_fusion.2), calls=%async_computation.2 | async-start | bytes 4194304 | tf_op jit(solution)/shard_map/all_to_all | solution.py:16
  193.6 6.7 %concatenate.23 = f32[128,9218]{1,0:T(8,128)} concatenate(f32[128,257]{1,0:T(8,128)S(1)} %broadcast.29, f32[128,256]{1,0:T(8,128)S(1)} %collective-permute-done.10, f32[128,8192]{1,0:T(8,128)} %copy-done.5, f32[128,513]{1,0:T(8,128)S(1)} %broadcast.30), dimensions={1} | concatenate | bytes 9439232 | tf_op jit(solution)/shard_map/concatenate | solution.py:46
  200.3 1.8 dynamic_update_slice.23
  202.2 13.2 %all-to-all-done.2 = bf16[2,128,4096]{2,1,0:T(8,128)(2,1)} async-done(((bf16[2,128,4096]{2,1,0:T(8,128)(2,1)}), bf16[2,128,4096]{2,1,0:T(8,128)(2,1)}, u32[]{:S(2)}, u32[]{:S(2)}) %all-to-all-start.2) | async-done | bytes 2097184 | tf_op jit(solution)/shard_map/all_to_all | solution.py:16
  215.4 3.8 %all-to-all-start.3 = ((bf16[2,128,4096]{2,1,0:T(8,128)(2,1)}), bf16[2,128,4096]{2,1,0:T(8,128)(2,1)S(1)}, u32[]{:S(2)}, u32[]{:S(2)}) async-start(bf16[2,128,4096]{2,1,0:T(8,128)(2,1)} %pad_maximum_fusion.3), calls=%async_computation.3 | async-start | bytes 4194304 | tf_op jit(solution)/shard_map/all_to_all | solution.py:16
  219.1 18.9 %fusion.7 = bf16[128,8192]{1,0:T(8,128)(2,1)} fusion(f32[128,8192]{1,0:T(8,128)} %copy-done.1, f32[128,9218]{1,0:T(8,128)} %dynamic_update_slice.23, pred[8192]{0:T(1024)(128)(4,1)S(1)} %get-tuple-element.6, pred[8192]{0:T(1024)(128)(4,1)S(1)} %get-tuple-element.7, pred[8192]{0:T(1024)(128)(4,1)S(1)} %get-tuple-element.8, ...), kind=kLoop, calls=%fused_computation.14 | loop fusion | flops 18874368 | bytes 44105728 | tf_op jit(solution)/shard_map/convert_element_type | solution.py:71
  238.0 5.5 %all-to-all-done.3 = bf16[2,128,4096]{2,1,0:T(8,128)(2,1)S(1)} async-done(((bf16[2,128,4096]{2,1,0:T(8,128)(2,1)}), bf16[2,128,4096]{2,1,0:T(8,128)(2,1)S(1)}, u32[]{:S(2)}, u32[]{:S(2)}) %all-to-all-start.3) | async-done | bytes 2097184 | tf_op jit(solution)/shard_map/all_to_all | solution.py:16
  243.5 4.8 %all-to-all-start.4 = ((bf16[2,128,4096]{2,1,0:T(8,128)(2,1)}), bf16[2,128,4096]{2,1,0:T(8,128)(2,1)}, u32[]{:S(2)}, u32[]{:S(2)}) async-start(bf16[2,128,4096]{2,1,0:T(8,128)(2,1)} %pad_maximum_fusion.4), calls=%async_computation.4 | async-start | bytes 4194304 | tf_op jit(solution)/shard_map/all_to_all | solution.py:16
  248.3 1.7 slice_bitcast_fusion.1
  251.6 22.5 %all-to-all-done.4 = bf16[2,128,4096]{2,1,0:T(8,128)(2,1)} async-done(((bf16[2,128,4096]{2,1,0:T(8,128)(2,1)}), bf16[2,128,4096]{2,1,0:T(8,128)(2,1)}, u32[]{:S(2)}, u32[]{:S(2)}) %all-to-all-start.4) | async-done | bytes 2097184 | tf_op jit(solution)/shard_map/all_to_all | solution.py:16
  274.0 4.8 %all-to-all-start.5 = ((bf16[2,128,4096]{2,1,0:T(8,128)(2,1)}), bf16[2,128,4096]{2,1,0:T(8,128)(2,1)}, u32[]{:S(2)}, u32[]{:S(2)}) async-start(bf16[2,128,4096]{2,1,0:T(8,128)(2,1)} %pad_maximum_fusion.5), calls=%async_computation.5 | async-start | bytes 4194304 | tf_op jit(solution)/shard_map/all_to_all | solution.py:16
  278.9 2.4 fusion.64
  281.2 2.4 convolution_add_fusion.5
  283.7 4.4 %convolution_add_fusion.4 = f32[4096,256]{1,0:T(8,128)} fusion(f32[4096,256]{1,0:T(8,128)S(1)} %convolution_add_fusion.5, bf16[256,4096]{1,0:T(8,128)(2,1)} %bitcast.12, bf16[7,256,256]{2,1,0:T(8,128)(2,1)S(1)} %copy-done.7), kind=kOutput, calls=%fused_computation.6 | convolution fusion | flops 537919488 | bytes 10616832 | tf_op jit(solution)/shard_map/ip,io->po/dot_general | solution.py:76
  288.1 16.6 %all-to-all-done.5 = bf16[2,128,4096]{2,1,0:T(8,128)(2,1)} async-done(((bf16[2,128,4096]{2,1,0:T(8,128)(2,1)}), bf16[2,128,4096]{2,1,0:T(8,128)(2,1)}, u32[]{:S(2)}, u32[]{:S(2)}) %all-to-all-start.5) | async-done | bytes 2097184 | tf_op jit(solution)/shard_map/all_to_all | solution.py:16
  304.7 5.1 %all-to-all-start.6 = ((bf16[2,128,4096]{2,1,0:T(8,128)(2,1)}), bf16[2,128,4096]{2,1,0:T(8,128)(2,1)}, u32[]{:S(2)}, u32[]{:S(2)}) async-start(bf16[2,128,4096]{2,1,0:T(8,128)(2,1)} %pad_maximum_fusion.6), calls=%async_computation.6 | async-start | bytes 4194304 | tf_op jit(solution)/shard_map/all_to_all | solution.py:16
  309.8 3.0 convolution_add_fusion.3
  312.8 2.4 convolution_add_fusion.2
  315.2 4.4 %convolution_add_fusion.1 = f32[4096,256]{1,0:T(8,128)} fusion(f32[4096,256]{1,0:T(8,128)S(1)} %convolution_add_fusion.2, bf16[256,4096]{1,0:T(8,128)(2,1)} %bitcast.24, bf16[7,256,256]{2,1,0:T(8,128)(2,1)S(1)} %copy-done.7), kind=kOutput, calls=%fused_computation.3 | convolution fusion | flops 537919488 | bytes 10616832 | tf_op jit(solution)/shard_map/ip,io->po/dot_general | solution.py:76
  319.6 14.9 %all-to-all-done.6 = bf16[2,128,4096]{2,1,0:T(8,128)(2,1)} async-done(((bf16[2,128,4096]{2,1,0:T(8,128)(2,1)}), bf16[2,128,4096]{2,1,0:T(8,128)(2,1)}, u32[]{:S(2)}, u32[]{:S(2)}) %all-to-all-start.6) | async-done | bytes 2097184 | tf_op jit(solution)/shard_map/all_to_all | solution.py:16
  334.6 4.5 %fusion.3 = bf16[1,4096,256]{2,1,0:T(8,128)(2,1)} fusion(f32[4096,256]{1,0:T(8,128)} %convolution_add_fusion.1, bf16[256,4096]{1,0:T(8,128)(2,1)} %bitcast.28, f32[256]{0:T(256)S(1)} %copy-done.9, pred[4096]{0:T(1024)(128)(4,1)S(1)} %add_compare_fusion, bf16[7,256,256]{2,1,0:T(8,128)(2,1)S(1)} %copy-done.7), kind=kOutput, calls=%fused_computation.9 | convolution fusion | flops 541065216 | bytes 8524800 | tf_op jit(solution)/shard_map/ip,io->po/dot_general | solution.py:76
  (63 shorter events, 20.5 us)
Async XLA Ops:
  1.7 6.3 %copy-start.4 = (bf16[128,8192]{1,0:T(8,128)(2,1)S(1)}, bf16[128,8192]{1,0:T(8,128)(2,1)}, u32[]{:S(2)}) copy-start(bf16[128,8192]{1,0:T(8,128)(2,1)} %param.5) | copy-start | bytes 6291460
  3.2 153.7 %all-to-all-start = ((bf16[2,128,4096]{2,1,0:T(8,128)(2,1)}), bf16[2,128,4096]{2,1,0:T(8,128)(2,1)}, u32[]{:S(2)}, u32[]{:S(2)}) async-start(bf16[2,128,4096]{2,1,0:T(8,128)(2,1)} %pad_maximum_fusion), calls=%async_computation | async-start | bytes 4194304 | tf_op jit(solution)/shard_map/all_to_all | solution.py:16
  8.0 5.8 %copy-start.8 = (s32[8,8192]{1,0:T(8,128)S(1)}, s32[8,8192]{1,0:T(8,128)}, u32[]{:S(2)}) copy-start(s32[8,8192]{1,0:T(8,128)} %param.6) | copy-start | bytes 786436
  12.0 4.4 %collective-permute-start = (f32[128,256]{1,0:T(8,128)S(1)}, f32[128,256]{1,0:T(8,128)S(1)}, u32[]{:S(2)}, u32[]{:S(2)}) collective-permute-start(f32[128,256]{1,0:T(8,128)S(1)} %constant_dynamic-slice_fusion.5), channel_id=1, source_target_pairs={{0,1},{1,4},{4,5},{5,8},{8,9},{9,12},{12,13},{13,0},{2,3},{3,6},{6... | collective-permute-start | bytes 393224 | tf_op jit(solution)/shard_map/ppermute | solution.py:25
  12.1 8.7 %collective-permute-start.1 = (f32[128,256]{1,0:T(8,128)S(1)}, f32[128,256]{1,0:T(8,128)S(1)}, u32[]{:S(2)}, u32[]{:S(2)}) collective-permute-start(f32[128,256]{1,0:T(8,128)S(1)} %slice.341), channel_id=1, source_target_pairs={{0,13},{1,0},{4,1},{5,4},{8,5},{9,8},{12,9},{13,12},{2,15},{3,2},{... | collective-permute-start | bytes 393224 | tf_op jit(solution)/shard_map/ppermute | solution.py:25
  39.3 3.5 %copy-start.3 = (f32[128,8192]{1,0:T(8,128)}, f32[128,8192]{1,0:T(8,128)S(1)}, u32[]{:S(2)}) copy-start(f32[128,8192]{1,0:T(8,128)S(1)} %get-tuple-element.22) | copy-start | bytes 12582916
  39.6 4.4 %collective-permute-start.2 = (f32[128,256]{1,0:T(8,128)S(1)}, f32[128,256]{1,0:T(8,128)S(1)}, u32[]{:S(2)}, u32[]{:S(2)}) collective-permute-start(f32[128,256]{1,0:T(8,128)S(1)} %get-tuple-element.32), channel_id=1, source_target_pairs={{0,1},{1,4},{4,5},{5,8},{8,9},{9,12},{12,13},{13,0},{2,3},{3,6},{6... | collective-permute-start | bytes 393224 | tf_op jit(solution)/shard_map/ppermute | solution.py:25
  39.7 11.1 %collective-permute-start.3 = (f32[128,256]{1,0:T(8,128)S(1)}, f32[128,256]{1,0:T(8,128)S(1)}, u32[]{:S(2)}, u32[]{:S(2)}) collective-permute-start(f32[128,256]{1,0:T(8,128)S(1)} %get-tuple-element.31), channel_id=1, source_target_pairs={{0,13},{1,0},{4,1},{5,4},{8,5},{9,8},{12,9},{13,12},{2,15},{3,2},{... | collective-permute-start | bytes 393224 | tf_op jit(solution)/shard_map/ppermute | solution.py:25
  70.3 6.5 %copy-start.2 = (f32[128,8192]{1,0:T(8,128)}, f32[128,8192]{1,0:T(8,128)S(1)}, u32[]{:S(2)}) copy-start(f32[128,8192]{1,0:T(8,128)S(1)} %get-tuple-element.20) | copy-start | bytes 12582916
  73.6 4.4 %collective-permute-start.4 = (f32[128,256]{1,0:T(8,128)S(1)}, f32[128,256]{1,0:T(8,128)S(1)}, u32[]{:S(2)}, u32[]{:S(2)}) collective-permute-start(f32[128,256]{1,0:T(8,128)S(1)} %get-tuple-element.30), channel_id=1, source_target_pairs={{0,1},{1,4},{4,5},{5,8},{8,9},{9,12},{12,13},{13,0},{2,3},{3,6},{6... | collective-permute-start | bytes 393224 | tf_op jit(solution)/shard_map/ppermute | solution.py:25
  74.6 10.2 %collective-permute-start.5 = (f32[128,256]{1,0:T(8,128)S(1)}, f32[128,256]{1,0:T(8,128)S(1)}, u32[]{:S(2)}, u32[]{:S(2)}) collective-permute-start(f32[128,256]{1,0:T(8,128)S(1)} %get-tuple-element.29), channel_id=1, source_target_pairs={{0,13},{1,0},{4,1},{5,4},{8,5},{9,8},{12,9},{13,12},{2,15},{3,2},{... | collective-permute-start | bytes 393224 | tf_op jit(solution)/shard_map/ppermute | solution.py:25
  105.3 7.6 %copy-start = (f32[128,8192]{1,0:T(8,128)}, f32[128,8192]{1,0:T(8,128)S(1)}, u32[]{:S(2)}) copy-start(f32[128,8192]{1,0:T(8,128)S(1)} %get-tuple-element.18) | copy-start | bytes 12582916
  108.6 4.4 %collective-permute-start.6 = (f32[128,256]{1,0:T(8,128)S(1)}, f32[128,256]{1,0:T(8,128)S(1)}, u32[]{:S(2)}, u32[]{:S(2)}) collective-permute-start(f32[128,256]{1,0:T(8,128)S(1)} %get-tuple-element.28), channel_id=1, source_target_pairs={{0,1},{1,4},{4,5},{5,8},{8,9},{9,12},{12,13},{13,0},{2,3},{3,6},{6... | collective-permute-start | bytes 393224 | tf_op jit(solution)/shard_map/ppermute | solution.py:25
  111.4 8.4 %collective-permute-start.7 = (f32[128,256]{1,0:T(8,128)S(1)}, f32[128,256]{1,0:T(8,128)S(1)}, u32[]{:S(2)}, u32[]{:S(2)}) collective-permute-start(f32[128,256]{1,0:T(8,128)S(1)} %get-tuple-element.27), channel_id=1, source_target_pairs={{0,13},{1,0},{4,1},{5,4},{8,5},{9,8},{12,9},{13,12},{2,15},{3,2},{... | collective-permute-start | bytes 393224 | tf_op jit(solution)/shard_map/ppermute | solution.py:25
  140.5 7.9 %copy-start.1 = (f32[128,8192]{1,0:T(8,128)}, f32[128,8192]{1,0:T(8,128)S(1)}, u32[]{:S(2)}) copy-start(f32[128,8192]{1,0:T(8,128)S(1)} %get-tuple-element.16) | copy-start | bytes 12582916
  140.5 7.8 %collective-permute-start.8 = (f32[128,256]{1,0:T(8,128)S(1)}, f32[128,256]{1,0:T(8,128)S(1)}, u32[]{:S(2)}, u32[]{:S(2)}) collective-permute-start(f32[128,256]{1,0:T(8,128)S(1)} %get-tuple-element.26), channel_id=1, source_target_pairs={{0,1},{1,4},{4,5},{5,8},{8,9},{9,12},{12,13},{13,0},{2,3},{3,6},{6... | collective-permute-start | bytes 393224 | tf_op jit(solution)/shard_map/ppermute | solution.py:25
  145.1 10.0 %collective-permute-start.9 = (f32[128,256]{1,0:T(8,128)S(1)}, f32[128,256]{1,0:T(8,128)S(1)}, u32[]{:S(2)}, u32[]{:S(2)}) collective-permute-start(f32[128,256]{1,0:T(8,128)S(1)} %get-tuple-element.25), channel_id=1, source_target_pairs={{0,13},{1,0},{4,1},{5,4},{8,5},{9,8},{12,9},{13,12},{2,15},{3,2},{... | collective-permute-start | bytes 393224 | tf_op jit(solution)/shard_map/ppermute | solution.py:25
  156.9 30.1 %all-to-all-start.1 = ((bf16[2,128,4096]{2,1,0:T(8,128)(2,1)}), bf16[2,128,4096]{2,1,0:T(8,128)(2,1)}, u32[]{:S(2)}, u32[]{:S(2)}) async-start(bf16[2,128,4096]{2,1,0:T(8,128)(2,1)} %pad_maximum_fusion.1), calls=%async_computation.1 | async-start | bytes 4194304 | tf_op jit(solution)/shard_map/all_to_all | solution.py:16
  180.7 2.1 copy-start.5
  182.8 9.1 %copy-start.6 = (bf16[128,8192]{1,0:T(8,128)(2,1)S(1)}, bf16[128,8192]{1,0:T(8,128)(2,1)}, u32[]{:S(2)}) copy-start(bf16[128,8192]{1,0:T(8,128)(2,1)} %get-tuple-element.13) | copy-start | bytes 6291460
  182.8 10.8 %collective-permute-start.10 = (f32[128,256]{1,0:T(8,128)S(1)}, f32[128,256]{1,0:T(8,128)S(1)}, u32[]{:S(2)}, u32[]{:S(2)}) collective-permute-start(f32[128,256]{1,0:T(8,128)S(1)} %get-tuple-element.24), channel_id=1, source_target_pairs={{0,1},{1,4},{4,5},{5,8},{8,9},{9,12},{12,13},{13,0},{2,3},{3,6},{6... | collective-permute-start | bytes 393224 | tf_op jit(solution)/shard_map/ppermute | solution.py:25
  187.1 13.2 %collective-permute-start.11 = (f32[128,256]{1,0:T(8,128)S(1)}, f32[128,256]{1,0:T(8,128)S(1)}, u32[]{:S(2)}, u32[]{:S(2)}) collective-permute-start(f32[128,256]{1,0:T(8,128)S(1)} %get-tuple-element.23), channel_id=1, source_target_pairs={{0,13},{1,0},{4,1},{5,4},{8,5},{9,8},{12,9},{13,12},{2,15},{3,2},{... | collective-permute-start | bytes 393224 | tf_op jit(solution)/shard_map/ppermute | solution.py:25
  187.1 28.3 %all-to-all-start.2 = ((bf16[2,128,4096]{2,1,0:T(8,128)(2,1)}), bf16[2,128,4096]{2,1,0:T(8,128)(2,1)}, u32[]{:S(2)}, u32[]{:S(2)}) async-start(bf16[2,128,4096]{2,1,0:T(8,128)(2,1)} %pad_maximum_fusion.2), calls=%async_computation.2 | async-start | bytes 4194304 | tf_op jit(solution)/shard_map/all_to_all | solution.py:16
  215.4 28.2 %all-to-all-start.3 = ((bf16[2,128,4096]{2,1,0:T(8,128)(2,1)}), bf16[2,128,4096]{2,1,0:T(8,128)(2,1)S(1)}, u32[]{:S(2)}, u32[]{:S(2)}) async-start(bf16[2,128,4096]{2,1,0:T(8,128)(2,1)} %pad_maximum_fusion.3), calls=%async_computation.3 | async-start | bytes 4194304 | tf_op jit(solution)/shard_map/all_to_all | solution.py:16
  243.5 30.5 %all-to-all-start.4 = ((bf16[2,128,4096]{2,1,0:T(8,128)(2,1)}), bf16[2,128,4096]{2,1,0:T(8,128)(2,1)}, u32[]{:S(2)}, u32[]{:S(2)}) async-start(bf16[2,128,4096]{2,1,0:T(8,128)(2,1)} %pad_maximum_fusion.4), calls=%async_computation.4 | async-start | bytes 4194304 | tf_op jit(solution)/shard_map/all_to_all | solution.py:16
  250.0 28.9 %copy-start.7 = (bf16[7,256,256]{2,1,0:T(8,128)(2,1)S(1)}, bf16[7,256,256]{2,1,0:T(8,128)(2,1)}, u32[]{:S(2)}) copy-start(bf16[7,256,256]{2,1,0:T(8,128)(2,1)} %param.8) | copy-start | bytes 2752516
  274.0 30.7 %all-to-all-start.5 = ((bf16[2,128,4096]{2,1,0:T(8,128)(2,1)}), bf16[2,128,4096]{2,1,0:T(8,128)(2,1)}, u32[]{:S(2)}, u32[]{:S(2)}) async-start(bf16[2,128,4096]{2,1,0:T(8,128)(2,1)} %pad_maximum_fusion.5), calls=%async_computation.5 | async-start | bytes 4194304 | tf_op jit(solution)/shard_map/all_to_all | solution.py:16
  304.7 29.9 %all-to-all-start.6 = ((bf16[2,128,4096]{2,1,0:T(8,128)(2,1)}), bf16[2,128,4096]{2,1,0:T(8,128)(2,1)}, u32[]{:S(2)}, u32[]{:S(2)}) async-start(bf16[2,128,4096]{2,1,0:T(8,128)(2,1)} %pad_maximum_fusion.6), calls=%async_computation.6 | async-start | bytes 4194304 | tf_op jit(solution)/shard_map/all_to_all | solution.py:16
  315.2 19.4 %copy-start.9 = (f32[256]{0:T(256)S(1)}, f32[256]{0:T(256)}, u32[]{:S(2)}) copy-start(f32[256]{0:T(256)} %param.9) | copy-start | bytes 3076
